TPU v7x, 256 devices: a whole 4x4x8 slice. The times are simulated.
256 devices in a mesh: seq: 64 (over y, z, core), fsdp: 4 (over x).
Axes of the slice: x: 4, y: 4, z: 8, core: 2. Of those that a mesh axis runs over, the one named last changes fastest.
Arguments:
- queries: bfloat16 [16384, 2048], P('seq', 'fsdp'), may hold values from -2.5 to 2.5
- keys_values: bfloat16 [16384, 512], P('seq', 'fsdp'), may hold values from -2.5 to 2.5
- hidden_in: bfloat16 [16384, 2880], P(('seq', 'fsdp')), may hold values from -6 to 6
- out_weight: bfloat16 [2048, 2880], P('fsdp'), may hold values from -0.5 to 0.5
- norm_gain: float32 [2880], replicated, may hold values from 0.1 to 1.9
- router_weight: bfloat16 [2880, 64], replicated, may hold values from -0.109375 to 0.109375
- expert_ids: int32 [16384, 4], P(('seq', 'fsdp')), may hold values from 0 to 63, all different within a row; in each aligned block of 64 rows (0 to 63, 64 to 127, ...) at most 8 rows name the same one
- expert_gate: bfloat16 [64, 2880, 1536], P('seq', None, 'fsdp'), may hold values from -0.109375 to 0.109375
- expert_up: bfloat16 [64, 2880, 1536], P('seq', None, 'fsdp'), may hold values from -0.109375 to 0.109375
- expert_down: bfloat16 [64, 2880, 1536], P('seq', None, 'fsdp'), may hold values from -0.15625 to 0.15625
Outputs:
- layer_out: bfloat16 [16384, 2880], P(('seq', 'fsdp'))
Inputs may be any that keep to these rules, and one draw needn't show every extreme that they name: `expert_ids`: A row names 4 different experts. Within the rows of one device (aligned blocks of 64 rows) no expert is named by more than 8 rows, a bound that some block reaches.
All inputs are finite; a program needn't handle non-finite values.
Results may differ from a plain program's by a relative error of at most 0.0075.
Values may be sent and summed in bfloat16 or wider, within the bound.
No kernel may reach another device: no remote copies, remote signals or barrier semaphores. Data moves between devices by JAX's collectives and lax.ppermute only.
A program may use at most 128 MiB of HBM per device.

v0:
```python
import math

import jax
import jax.numpy as jnp
from jax import lax
from jax.sharding import PartitionSpec as P

D = 2880
HD = 64
WINDOW = 128
TOPK = 4


def in_one_piece(arrays, axis, dim, along):
    widths = [a.shape[along] for a in arrays]
    both = jnp.concatenate(arrays, axis=along)
    result = lax.all_gather(both, axis, axis=dim, tiled=True)
    return tuple(jnp.split(result, [sum(widths[:k]) for k in range(1, len(widths))], axis=along))


def shifted(shard, axis, by):
    count = lax.axis_size(axis)
    pairs = [(i, i + by) for i in range(count) if 0 <= i + by < count]
    return lax.ppermute(shard, axis, pairs)


def in_blocks(shard, dim, count):
    before, after = (shard.shape[:dim], shard.shape[dim + 1 :])
    return jnp.moveaxis(shard.reshape(*before, count, -1, *after), dim, 0)


def sum_at_owner(shard, axis, dim):
    blocks = in_blocks(shard, dim, lax.axis_size(axis))
    arrived = lax.all_to_all(blocks, axis, split_axis=0, concat_axis=0, tiled=True)
    return arrived.sum(axis=0)


def swiglu_piece(row_block, gate_part, up_part):
    gate_vals = jnp.dot(row_block, gate_part, preferred_element_type=jnp.float32)
    up_vals = jnp.dot(row_block, up_part, preferred_element_type=jnp.float32)
    return (gate_vals * jax.nn.sigmoid(1.702 * gate_vals) * (up_vals + 1.0)).astype(jnp.bfloat16)


def down_piece(hidden, down_part):
    return jnp.einsum("nk,dk->nd", hidden, down_part, preferred_element_type=jnp.float32)


def expert_rows(row_block, gate_part, up_part, down_part):
    pieces = in_one_piece((gate_part, up_part, down_part), "fsdp", 1, 0)
    hidden = swiglu_piece(row_block, pieces[0], pieces[1])
    combined = down_piece(hidden, pieces[2])
    return combined.astype(jnp.bfloat16)


def per_device(
    queries,
    keys_values,
    hidden_in,
    out_weight,
    norm_gain,
    router_weight,
    expert_ids,
    expert_gate,
    expert_up,
    expert_down,
):
    tok_dev = queries.shape[0]
    kv_heads = keys_values.shape[1] // (2 * HD)
    heads_local = queries.shape[1] // HD
    groups = heads_local // kv_heads
    key_rim = shifted(keys_values[tok_dev - WINDOW :], "seq", 1)
    extended = jnp.concatenate([key_rim, keys_values], axis=0).reshape(
        WINDOW + tok_dev, kv_heads, 2, HD
    )
    grouped = queries.reshape(tok_dev, kv_heads, groups, HD)
    scores = jnp.einsum(
        "tkgd,skd->kgts", grouped, extended[:, :, 0], preferred_element_type=jnp.float32
    ) * (1.0 / math.sqrt(HD))
    first_pos = lax.axis_index("seq") * tok_dev
    query_pos = first_pos + jnp.arange(tok_dev, dtype=jnp.int32)
    key_pos = first_pos - WINDOW + jnp.arange(WINDOW + tok_dev, dtype=jnp.int32)
    offset = query_pos[:, None] - key_pos[None, :]
    allowed = (offset >= 0) & (offset <= WINDOW) & (key_pos[None, :] >= 0)
    raised = jnp.where(allowed, jnp.exp(scores), 0.0)
    attn_probs = (raised / jnp.sum(raised, axis=-1, keepdims=True)).astype(jnp.bfloat16)
    mixed_heads = jnp.einsum(
        "kgts,skd->tkgd", attn_probs, extended[:, :, 1], preferred_element_type=jnp.float32
    )
    attended = mixed_heads.astype(jnp.bfloat16).reshape(tok_dev, heads_local * HD)
    partial_value = jnp.dot(attended, out_weight, preferred_element_type=jnp.float32)
    rows_dev = tok_dev // lax.axis_size("fsdp")
    projected = sum_at_owner(partial_value, "fsdp", 0)
    stream = (hidden_in.astype(jnp.float32) + projected).astype(jnp.bfloat16)
    stream = lax.optimization_barrier(stream)
    stream_wide = stream.astype(jnp.float32)
    inverse = lax.rsqrt(jnp.mean(stream_wide * stream_wide, axis=1, keepdims=True) + 1e-05)
    normed = (stream_wide * inverse * norm_gain).astype(jnp.bfloat16)
    experts = router_weight.shape[1]
    logits = jnp.dot(normed, router_weight, preferred_element_type=jnp.float32)
    chosen = expert_ids[:, :, None] == jnp.arange(experts, dtype=jnp.int32)[None, None, :]
    picked = jnp.sum(jnp.where(chosen, logits[:, None, :], 0.0), axis=2)
    raised_gates = jnp.exp(picked)
    gates = raised_gates / jnp.sum(raised_gates, axis=1, keepdims=True)
    flat_ids = expert_ids.reshape(-1)
    onehot = (flat_ids[:, None] == jnp.arange(experts, dtype=jnp.int32)[None, :]).astype(jnp.int32)
    running = jnp.cumsum(onehot, axis=0, dtype=jnp.int32) - onehot
    slot_ids = jnp.sum(running * onehot, axis=1, dtype=jnp.int32)
    capacity = 2 * tok_dev * TOPK // (lax.axis_size("fsdp") * experts)
    sources = jnp.repeat(normed, TOPK, axis=0)
    outgoing = jnp.zeros((experts, capacity, D), jnp.bfloat16).at[flat_ids, slot_ids].set(sources)
    owners = lax.axis_size("seq")
    per_owner = experts // owners
    outgoing = outgoing.reshape(owners, per_owner, capacity, D)
    received = lax.all_to_all(outgoing, "seq", split_axis=0, concat_axis=0, tiled=True)
    items_now = received.shape[2]
    row_block = received[:, 0].reshape(owners * items_now, D)
    answer = expert_rows(row_block, expert_gate[0], expert_up[0], expert_down[0])
    results = [answer.reshape(owners, items_now, D)]
    processed = jnp.stack(results, axis=1)
    returned = lax.all_to_all(processed, "seq", split_axis=0, concat_axis=0, tiled=True)
    return_table = returned.reshape(experts * capacity, D)
    fetched = (
        return_table[flat_ids * capacity + slot_ids].astype(jnp.float32).reshape(rows_dev, TOPK, D)
    )
    expert_sum = jnp.sum(fetched * gates[:, :, None], axis=1)
    return (stream_wide + expert_sum).astype(jnp.bfloat16)


def solution(mesh):
    return jax.shard_map(
        per_device,
        mesh=mesh,
        in_specs=(
            P("seq", "fsdp"),
            P("seq", "fsdp"),
            P(("seq", "fsdp"), None),
            P("fsdp", None),
            P(),
            P(),
            P(("seq", "fsdp"), None),
            P("seq", None, "fsdp"),
            P("seq", None, "fsdp"),
            P("seq", None, "fsdp"),
        ),
        out_specs=P(("seq", "fsdp"), None),
        check_vma=False,
    )
```

profile of v0, /device:TPU:1, one launch (start us, length us, event | category | flops | bytes accessed | tf_op | source)
XLA Modules:
  0.0 421.8 jit_solution(3089226141096706860)
XLA Ops:
  6.5 10.1 %pad_maximum_fusion = bf16[8640,384]{1,0:T(8,128)(2,1)} fusion(bf16[2880,384]{1,0:T(8,128)(2,1)} %bitcast.93, bf16[2880,384]{1,0:T(8,128)(2,1)} %bitcast.94, bf16[2880,384]{1,0:T(8,128)(2,1)} %bitcast.95), kind=kLoop, calls=%fused_computation.8 | loop fusion | flops 19906560 | bytes 13271040 | tf_op jit(solution)/shard_map/concatenate | solution.py:16
  16.7 0.8 copy-done.5
  17.5 0.6 slice.15
  18.1 4.9 %collective-permute-start = (bf16[128,128]{1,0:T(8,128)(2,1)}, bf16[128,128]{1,0:T(8,128)(2,1)}, u32[]{:S(2)}, u32[]{:S(2)}) collective-permute-start(bf16[128,128]{1,0:T(8,128)(2,1)} %slice.15), channel_id=1, source_target_pairs={{0,4},{4,8},{8,12},{12,16},{16,20},{20,24},{24,28},{28,32},{32,36}... | collective-permute-start | bytes 98312 | tf_op jit(solution)/shard_map/ppermute | solution.py:24
  23.1 0.8 fusion.45
  24.0 0.3 collective-permute-done
  24.3 0.8 pad_maximum_fusion.1
  25.1 0.8 copy.38
  25.9 1.8 fusion.28
  27.7 1.6 fusion.36
  29.2 1.2 reshape.204
  30.5 3.5 fusion.22
  34.0 4.1 all-to-all-start
  38.6 0.6 reduce-window.6
  39.5 64.4 %all-to-all-done = f32[4,64,2880]{2,1,0:T(8,128)S(1)} async-done(((f32[4,64,2880]{2,1,0:T(8,128)}), f32[4,64,2880]{2,1,0:T(8,128)S(1)}, u32[]{:S(2)}, u32[]{:S(2)}) %all-to-all-start) | async-done | bytes 2949152 | tf_op jit(solution)/shard_map/all_to_all | solution.py:34
  104.0 1.1 reduce_sum.66
  105.1 1.3 add_convert_fusion
  106.7 0.4 broadcast_in_dim.27
  107.1 1.6 reshape.197
  109.0 40.6 %scatter_fusion = bf16[64,8,2880]{2,1,0:T(8,128)(2,1)S(1)} fusion(bf16[64,8,2880]{2,1,0:T(8,128)(2,1)S(1)} %broadcast_in_dim.26, s32[256]{0:T(256)S(1)} %bitcast.91, bf16[256,2880]{1,0:T(8,128)(2,1)} %reshape.197), kind=kCustom, calls=%fused_computation.1 | custom fusion | bytes 4425728 | tf_op jit(solution)/shard_map/scatter | solution.py:110
  149.6 86.4 %all_to_all.15 = bf16[64,1,8,2880]{3,2,1,0:T(8,128)(2,1)} all-to-all(bf16[64,1,8,2880]{3,2,1,0:T(8,128)(2,1)S(1)} %bitcast.89), channel_id=1, replica_groups=mesh['seq'=64,'fsdp'=4] {'seq'}, dimensions={0} | all-to-all | bytes 5898240 | tf_op jit(solution)/shard_map/all_to_all | solution.py:114
  236.1 52.1 %all-gather.2.cloned.1.call-done = bf16[8640,1536]{1,0:T(8,128)(2,1)} async-done(((bf16[8640,384]{1,0:T(8,128)(2,1)}), bf16[8640,1536]{1,0:T(8,128)(2,1)}) %all-gather.2.cloned.1.call-update) | async-done | bytes 26542096 | tf_op jit(solution)/shard_map/all_gather | solution.py:17
  288.2 10.4 %fusion.4 = f32[512,1536]{1,0:T(8,128)} fusion(bf16[8640,1536]{1,0:T(8,128)(2,1)} %all-gather.2.cloned.1.call-done, bf16[64,1,8,2880]{3,2,1,0:T(8,128)(2,1)} %all_to_all.15), kind=kOutput, calls=%fused_computation.6 | convolution fusion | flops 4529848320 | bytes 15007744 | tf_op jit(solution)/shard_map/dot_general | solution.py:39
  298.5 18.4 %fusion.6 = bf16[512,2880]{0,1:T(8,128)(2,1)} fusion(bf16[8640,1536]{1,0:T(8,128)(2,1)} %all-gather.2.cloned.1.call-done, bf16[64,1,8,2880]{3,2,1,0:T(8,128)(2,1)S(1)} %copy-done.3, f32[512,1536]{1,0:T(8,128)} %fusion.4), kind=kOutput, calls=%fused_computation.9 | convolution fusion | flops 9067462656 | bytes 26738688 | tf_op jit(solution)/shard_map/nk,dk->nd/dot_general | solution.py:45
  316.9 4.6 %copy.46 = bf16[512,2880]{1,0:T(8,128)(2,1)} copy(bf16[512,2880]{0,1:T(8,128)(2,1)} %fusion.6) | data formatting | bytes 5898240 | tf_op jit(solution)/shard_map/convert_element_type | solution.py:52
  321.4 11.3 %all-to-all-start.2 = ((bf16[64,1,8,2880]{3,2,1,0:T(8,128)(2,1)}), bf16[64,1,8,2880]{3,2,1,0:T(8,128)(2,1)S(1)}, u32[]{:S(2)}, u32[]{:S(2)}) async-start(bf16[64,1,8,2880]{3,2,1,0:T(8,128)(2,1)} %bitcast.92), calls=%async_computation.2 | async-start | bytes 6029312 | tf_op jit(solution)/shard_map/all_to_all | solution.py:120
  332.8 1.4 fusion.56
  334.5 69.0 %all-to-all-done.2 = bf16[64,1,8,2880]{3,2,1,0:T(8,128)(2,1)S(1)} async-done(((bf16[64,1,8,2880]{3,2,1,0:T(8,128)(2,1)}), bf16[64,1,8,2880]{3,2,1,0:T(8,128)(2,1)S(1)}, u32[]{:S(2)}, u32[]{:S(2)}) %all-to-all-start.2) | async-done | bytes 2949152 | tf_op jit(solution)/shard_map/all_to_all | solution.py:120
  403.4 2.7 gather_fusion
  406.1 4.1 reshape.186
  410.2 4.0 multiply_reduce_fusion
  414.1 0.8 fusion.42
  (44 shorter events, 1.8 us)
Async XLA Ops:
  6.5 24.0 %copy-start = (bf16[512,2880]{0,1:T(8,128)(2,1)S(1)}, bf16[512,2880]{0,1:T(8,128)(2,1)}, u32[]{:S(2)}) copy-start(bf16[512,2880]{0,1:T(8,128)(2,1)} %param.13) | copy-start | bytes 8847364
  6.5 281.6 %all-gather.2.cloned.1.call-start = ((), (), s32[]{:S(2)}) async-start(), calls=%async_computation.3 | async-start | bytes 33177600 | tf_op jit(solution)/shard_map/all_gather | solution.py:17
  16.6 0.8 copy-start.5
  16.6 7.2 %copy-start.4 = (bf16[256,512]{1,0:T(8,128)(2,1)S(1)}, bf16[256,512]{1,0:T(8,128)(2,1)}, u32[]{:S(2)}) copy-start(bf16[256,512]{1,0:T(8,128)(2,1)} %param.10) | copy-start | bytes 786436
  18.1 6.3 %collective-permute-start = (bf16[128,128]{1,0:T(8,128)(2,1)}, bf16[128,128]{1,0:T(8,128)(2,1)}, u32[]{:S(2)}, u32[]{:S(2)}) collective-permute-start(bf16[128,128]{1,0:T(8,128)(2,1)} %slice.15), channel_id=1, source_target_pairs={{0,4},{4,8},{8,12},{12,16},{16,20},{20,24},{24,28},{28,32},{32,36}... | collective-permute-start | bytes 98312 | tf_op jit(solution)/shard_map/ppermute | solution.py:24
  24.0 3.6 copy-start.6
  25.9 1.8 copy-start.7
  34.0 4.1 copy-start.9
  34.0 70.0 %all-to-all-start = ((f32[4,64,2880]{2,1,0:T(8,128)}), f32[4,64,2880]{2,1,0:T(8,128)S(1)}, u32[]{:S(2)}, u32[]{:S(2)}) async-start(f32[4,64,2880]{2,1,0:T(8,128)} %fusion.22), calls=%async_computation | async-start | bytes 6029312 | tf_op jit(solution)/shard_map/all_to_all | solution.py:34
  38.1 68.4 %copy-start.8 = (f32[2880]{0:T(1024)S(1)}, f32[2880]{0:T(1024)}, u32[]{:S(2)}) copy-start(f32[2880]{0:T(1024)} %param.14) | copy-start | bytes 34564
  106.7 2.0 copy-start.2
  236.1 62.5 %copy-start.3 = (bf16[64,1,8,2880]{3,2,1,0:T(8,128)(2,1)S(1)}, bf16[64,1,8,2880]{3,2,1,0:T(8,128)(2,1)}, u32[]{:S(2)}) copy-start(bf16[64,1,8,2880]{3,2,1,0:T(8,128)(2,1)} %all_to_all.15) | copy-start | bytes 8847364
  321.4 82.0 %all-to-all-start.2 = ((bf16[64,1,8,2880]{3,2,1,0:T(8,128)(2,1)}), bf16[64,1,8,2880]{3,2,1,0:T(8,128)(2,1)S(1)}, u32[]{:S(2)}, u32[]{:S(2)}) async-start(bf16[64,1,8,2880]{3,2,1,0:T(8,128)(2,1)} %bitcast.92), calls=%async_computation.2 | async-start | bytes 6029312 | tf_op jit(solution)/shard_map/all_to_all | solution.py:120
  406.1 8.9 %copy-start.1 = (bf16[512,2880]{0,1:T(8,128)(2,1)S(1)}, bf16[512,2880]{0,1:T(8,128)(2,1)}, u32[]{:S(2)}) copy-start(bf16[512,2880]{0,1:T(8,128)(2,1)} %param.13) | copy-start | bytes 8847364
Sparse Core Ops, SparseCore 0:
  16.8 271.3 all-gather.1
where the time goes:
time: 423 us; the launch traced here: 422 us
  waiting for transfers between devices  186 us (44%)
  blocking collectives  86.4 us (20%)
  local copies, waits for them, and re-layouts  58.5 us (14%)
  matrix products  36.9 us (9%)
  starting transfers between devices  20.4 us (5%)
  other arithmetic  20.2 us (5%)
  between operations  13.6 us (3%)
    all_to_all x1, blocking collectives, per_device(): lax.all_to_all(outgoing, 'seq', split_axis=0, concat_axis=0, tiled=True)  86.4 us
    all_to_all x1, waiting for transfers between devices, per_device(): lax.all_to_all(processed, 'seq', split_axis=0, concat_axis=0, tiled=True)  69 us
    all_to_all x1, waiting for transfers between devices, sum_at_owner(): lax.all_to_all(blocks, axis, split_axis=0, concat_axis=0, tiled=True)  64.4 us
    all_gather x1, waiting for transfers between devices, in_one_piece(): result = lax.all_gather(both, axis, axis=dim, tiled=True)  52.1 us
    scatter x1, local copies, waits for them, and re-layouts, per_device(): jnp.zeros((experts, capacity, D), jnp.bfloat16).at[flat_ids, slot_ids]  40.6 us
    dot_general x1, matrix products, down_piece(): jnp.einsum('nk,dk->nd', hidden, down_part, preferred_element_type=jnp.flo...  18.4 us
    all_to_all x1, starting transfers between devices, per_device(): lax.all_to_all(processed, 'seq', split_axis=0, concat_axis=0, tiled=True)  11.3 us
    dot_general x1, matrix products, swiglu_piece(): jnp.dot(row_block, gate_part, preferred_element_type=jnp.float32)  10.4 us
  transfers between devices with their start and end apart: 4, of which 4 were waited for; matrix products, arithmetic and copies ran while one was open for 14% of the time, Pallas kernels for 0%

commit v1 on v0

v1 whole, which is shorter than its diff:
```python
import functools
import math

import jax
import jax.numpy as jnp
from jax import lax
from jax.experimental import pallas as pl
from jax.experimental.pallas import tpu as pltpu
from jax.sharding import PartitionSpec as P

D = 2880
HD = 64
WINDOW = 128
TOPK = 4
SLOTS = 8
EXPERTS = 64
CHUNKS = 2
PER = SLOTS // CHUNKS
F32 = jnp.float32
BF16 = jnp.bfloat16
NT = (((1,), (1,)), ((), ()))
TN = (((0,), (0,)), ((), ()))
VMEM = pl.BlockSpec(memory_space=pltpu.VMEM)
SMEM = pl.BlockSpec(memory_space=pltpu.SMEM)
ANY = pl.BlockSpec(memory_space=pl.ANY)
BESIDE_WEIGHTS = [(0, 3), (3, 0), (1, 2), (2, 1)]
BESIDE_ROWS = [(0, 1), (1, 0), (2, 3), (3, 2)]


def call(body, outs, in_specs, scratch=(), flops=0, nbytes=0, limit=48):
    return pl.pallas_call(
        body,
        out_shape=outs,
        in_specs=in_specs,
        out_specs=jax.tree.map(lambda _: VMEM, outs),
        scratch_shapes=list(scratch),
        compiler_params=pltpu.CompilerParams(vmem_limit_bytes=limit << 20),
        cost_estimate=pl.CostEstimate(flops=flops, bytes_accessed=nbytes, transcendentals=0),
    )


def attention_body(place, q_ref, kv_ref, rim_ref, ow_ref, own_ref, to1, to2, to3, mixed):
    first, x = place[0] == 0, place[1]
    ext = jnp.concatenate([rim_ref[...], kv_ref[...]], axis=0)
    keys, values = ext[:, :HD], ext[:, HD:]
    row = lax.broadcasted_iota(jnp.int32, (WINDOW, 2 * WINDOW), 0)
    col = lax.broadcasted_iota(jnp.int32, (WINDOW, 2 * WINDOW), 1)
    band = (col >= row) & (col <= row + WINDOW)
    for b in range(2):
        allowed = band
        if b == 0:
            allowed = band & ((col >= WINDOW) | jnp.logical_not(first))
        k = keys[b * WINDOW : b * WINDOW + 2 * WINDOW]
        v = values[b * WINDOW : b * WINDOW + 2 * WINDOW]
        heads = []
        for h in range(q_ref.shape[1] // HD):
            q = q_ref[b * WINDOW : (b + 1) * WINDOW, h * HD : (h + 1) * HD]
            scores = lax.dot_general(q, k, NT, preferred_element_type=F32) * (1.0 / math.sqrt(HD))
            raised = jnp.where(allowed, jnp.exp(scores), 0.0)
            probs = (raised / jnp.sum(raised, axis=-1, keepdims=True)).astype(BF16)
            heads.append(jnp.dot(probs, v, preferred_element_type=F32))
        attended = jnp.concatenate(heads, axis=1).astype(BF16)
        for half in range(2):
            place_of = lax.rem(2 * b + half - x + 4, 4) * 64
            mixed[pl.ds(pl.multiple_of(place_of, 64), 64), :] = attended[half * 64 : half * 64 + 64]
    out = jnp.dot(mixed[...], ow_ref[...], preferred_element_type=F32)
    own_ref[...] = out[:64]
    to1[...] = out[64:128].astype(BF16)
    to2[...] = out[128:192].astype(BF16)
    to3[...] = out[192:].astype(BF16)


def norm_body(own, r1, r2, r3, hid, gain, pick0, pick1, stream_ref, normed_ref, out0, out1):
    projected = own[...] + r1[...].astype(F32) + r2[...].astype(F32) + r3[...].astype(F32)
    stream = (hid[...].astype(F32) + projected).astype(BF16)
    stream_ref[...] = stream
    wide = stream.astype(F32)
    inverse = lax.rsqrt(jnp.mean(wide * wide, axis=1, keepdims=True) + 1e-05)
    normed = (wide * inverse * gain[...]).astype(BF16)
    normed_ref[...] = normed
    out0[...] = jnp.dot(pick0[...], normed, preferred_element_type=F32).astype(BF16)
    out1[...] = jnp.dot(pick1[...], normed, preferred_element_type=F32).astype(BF16)


def gates_body(normed, router, chosen_t, spread, pick0, pick1, mix0, mix1):
    logits = lax.dot_general(router[...], normed[...], (((0,), (1,)), ((), ())), preferred_element_type=F32)
    raised = jnp.where(chosen_t[...] > 0.5, jnp.exp(logits), 0.0)
    gates = raised / jnp.sum(raised, axis=0, keepdims=True)
    rows = jnp.dot(spread[...], gates, preferred_element_type=F32, precision=lax.Precision.HIGHEST)
    for pick, mix in ((pick0, mix0), (pick1, mix1)):
        weight = pick[...].astype(F32) * rows
        high = weight.astype(BF16)
        low = (weight - high.astype(F32)).astype(BF16)
        mix[...] = jnp.concatenate([high, low], axis=1)


def hidden_body(xo, xp, g0, u0, g1, u1, ho, hp, vx, vw, sems):
    copies = [pltpu.make_async_copy(src, vx.at[i], sems.at[i]) for i, src in enumerate((xo, xp))]
    copies += [pltpu.make_async_copy(src, vw.at[i], sems.at[2 + i]) for i, src in enumerate((g0, u0, g1, u1))]
    for c in copies:
        c.start()
    width = g0.shape[1]
    copies[0].wait()
    copies[1].wait()
    for part in range(2):
        copies[2 + 2 * part].wait()
        copies[3 + 2 * part].wait()
        for i, h_ref in ((1, hp), (0, ho)):
            gate = jnp.dot(vx[i], vw[2 * part], preferred_element_type=F32)
            up = jnp.dot(vx[i], vw[2 * part + 1], preferred_element_type=F32)
            act = gate * jax.nn.sigmoid(1.702 * gate) * (up + 1.0)
            h_ref[:, part * width : (part + 1) * width] = act.astype(BF16)


def down_body(ho, hr, d0, d1, d2, d3, out, vw, acc, sems):
    copies = [pltpu.make_async_copy(src, vw.at[i], sems.at[i]) for i, src in enumerate((d0, d1, d2, d3))]
    for c in copies:
        c.start()
    width = d0.shape[1]
    for i in range(4):
        copies[i].wait()
        h = (ho, hr)[i // 2][:, (i % 2) * width : (i % 2 + 1) * width]
        term = lax.dot_general(h, vw[i], NT, preferred_element_type=F32)
        if i == 0:
            acc[...] = term
        elif i < 3:
            acc[...] += term
        else:
            out[...] = (acc[...] + term).astype(BF16)


def combine_body(stream, mix0, mix1, ret0, ret1, out):
    both = lax.dot_general(mix0[...], ret0[...], TN, preferred_element_type=F32)
    both += lax.dot_general(mix1[...], ret1[...], TN, preferred_element_type=F32)
    out[...] = (stream[...].astype(F32) + both[:64] + both[64:]).astype(BF16)


def shape(*dims, dtype=BF16):
    return jax.ShapeDtypeStruct(dims, dtype)


def per_device(
    queries,
    keys_values,
    hidden_in,
    out_weight,
    norm_gain,
    router_weight,
    expert_ids,
    expert_gate,
    expert_up,
    expert_down,
):
    tok_dev = queries.shape[0]
    rows_dev = hidden_in.shape[0]
    gate, up, down = expert_gate[0], expert_up[0], expert_down[0]
    width = gate.shape[1]
    owners = lax.axis_size("seq")
    rows = owners * PER

    beside_w = functools.partial(lax.ppermute, axis_name="fsdp", perm=BESIDE_WEIGHTS)
    beside_r = functools.partial(lax.ppermute, axis_name="fsdp", perm=BESIDE_ROWS)

    def shift(a, by):
        return lax.ppermute(a, "fsdp", [(i, (i + by) % 4) for i in range(4)])

    key_rim = lax.ppermute(
        keys_values[tok_dev - WINDOW :], "seq", [(i, i + 1) for i in range(owners - 1)]
    )
    gate_w, up_w = beside_w(gate), beside_w(up)
    down_r = beside_r(down)
    down_w = beside_w(down)
    far_low = beside_w(down_r[: D // 2])
    far_high = beside_r(down_w[D // 2 :])
    down_x = jnp.concatenate([far_low, far_high], axis=0)

    chosen = jnp.any(
        expert_ids[:, :, None] == jnp.arange(EXPERTS, dtype=jnp.int32)[None, None, :], axis=1
    ).astype(F32)
    before = (jnp.arange(rows_dev)[:, None] < jnp.arange(rows_dev)[None, :]).astype(F32)
    rank_t = lax.dot_general(chosen, before, TN, preferred_element_type=F32)
    chosen_t = chosen.T
    picks = []
    for c in range(CHUNKS):
        slot = (c * PER + jnp.arange(PER)).astype(F32)[None, :, None]
        hit = (chosen_t[:, None, :] > 0.5) & (rank_t[:, None, :] == slot)
        picks.append(hit.astype(BF16).reshape(rows, rows_dev))
    spread = (jnp.arange(rows)[:, None] // PER == jnp.arange(EXPERTS)[None, :]).astype(F32)

    place = jnp.stack([lax.axis_index("seq"), lax.axis_index("fsdp")]).astype(jnp.int32)
    own, to1, to2, to3 = call(
        attention_body,
        (shape(rows_dev, D, dtype=F32),) + (shape(rows_dev, D),) * 3,
        [SMEM] + [VMEM] * 4,
        [pltpu.VMEM((tok_dev, queries.shape[1]), BF16)],
        flops=2 * tok_dev * 512 * D,
        nbytes=8 << 20,
    )(place, queries, keys_values, key_rim, out_weight)
    r1, r2, r3 = shift(to1, 1), shift(to2, 2), shift(to3, 3)
    stream, normed, out0, out1 = call(
        norm_body,
        (shape(rows_dev, D), shape(rows_dev, D), shape(rows, D), shape(rows, D)),
        [VMEM] * 8,
        flops=4 * rows * rows_dev * D,
        nbytes=6 << 20,
    )(own, r1, r2, r3, hidden_in, norm_gain[None, :], *picks)

    def exchange(a):
        return lax.all_to_all(
            a.reshape(owners, PER, D), "seq", split_axis=0, concat_axis=0, tiled=True
        ).reshape(rows, D)

    received = [exchange(out0), exchange(out1)]
    mix0, mix1 = call(
        gates_body,
        (shape(rows, 2 * rows_dev),) * 2,
        [VMEM] * 6,
        flops=2 * rows_dev * D * EXPERTS,
        nbytes=1 << 20,
    )(normed, router_weight, chosen_t, spread, *picks)

    returned = []
    for mine in received:
        theirs = beside_r(mine)
        hid_mine, hid_theirs = call(
            hidden_body,
            (shape(rows, 2 * width),) * 2,
            [ANY] * 6,
            [
                pltpu.VMEM((2, rows, D), BF16),
                pltpu.VMEM((4, D, width), BF16),
                pltpu.SemaphoreType.DMA((6,)),
            ],
            flops=16 * rows * D * width,
            nbytes=12 << 20,
        )(mine, theirs, gate, up, gate_w, up_w)
        hid_rest = beside_r(hid_theirs)
        answer = call(
            down_body,
            shape(rows, D),
            [VMEM] * 2 + [ANY] * 4,
            [
                pltpu.VMEM((4, D, width), BF16),
                pltpu.VMEM((rows, D), F32),
                pltpu.SemaphoreType.DMA((4,)),
            ],
            flops=8 * rows * D * width,
            nbytes=12 << 20,
        )(hid_mine, hid_rest, down, down_w, down_r, down_x)
        returned.append(exchange(answer))
    return call(
        combine_body,
        shape(rows_dev, D),
        [VMEM] * 5,
        flops=8 * rows * rows_dev * D,
        nbytes=4 << 20,
    )(stream, mix0, mix1, *returned)


def solution(mesh):
    return jax.shard_map(
        per_device,
        mesh=mesh,
        in_specs=(
            P("seq", "fsdp"),
            P("seq", "fsdp"),
            P(("seq", "fsdp"), None),
            P("fsdp", None),
            P(),
            P(),
            P(("seq", "fsdp"), None),
            P("seq", None, "fsdp"),
            P("seq", None, "fsdp"),
            P("seq", None, "fsdp"),
        ),
        out_specs=P(("seq", "fsdp"), None),
        check_vma=False,
    )
```

time: 423 us -> 390 us (0.922)
  blocking collectives: 86.4 us -> 0 us
  starting transfers between devices: 20.4 us -> 71 us
  matrix products: 36.9 us -> 0.2 us
  Pallas kernels: 0 us -> 35.1 us
  waiting for transfers between devices: 186 us -> 216 us
  other arithmetic: 20.2 us -> 1.12 us
  between operations: 13.6 us -> 0.64 us
    ppermute x1 -> x14, waiting for transfers between devices: 0.3 us -> 152 us  [the longest x2 59.6 us: per_device(): theirs = beside_r(mine)]
    all_to_all x1 -> x0, blocking collectives: 86.4 us -> none  [per_device(): lax.all_to_all(outgoing, 'seq', split_axis=0, concat_axis=0, tiled=True)]
    all_to_all x2 -> x4, waiting for transfers between devices: 133 us -> 63.2 us  [exchange(): lax.all_to_all(a.reshape(owners, PER, D), 'seq', split_axis=0, concat_axi...]
    all_gather x1 -> x0, waiting for transfers between devices: 52.1 us -> none  [in_one_piece(): result = lax.all_gather(both, axis, axis=dim, tiled=True)]
    scatter x1 -> x0, local copies, waits for them, and re-layouts: 40.6 us -> none  [per_device(): jnp.zeros((experts, capacity, D), jnp.bfloat16).at[flat_ids, slot_ids]]
    dot_general x6 -> x1, matrix products: 36.9 us -> 0.2 us  [per_device(): rank_t = lax.dot_general(chosen, before, TN, preferred_element_type=F32)]
    pallas_call x0 -> x8, Pallas kernels: none -> 35.1 us  [the longest x2 18.8 us: per_device(): call(hidden_body, (shape(rows, 2 * width),) * 2, [ANY] * 6, [pltpu.VMEM((...]
    reshape x2 -> x10, local copies, waits for them, and re-layouts: 1.74 us -> 30.2 us  [the longest x6 17.6 us: exchange(): return lax.all_to_all(a.reshape(owners, PER, D), 'seq', split_axis=0, con...]
  transfers between devices with their start and end apart: 4 -> 18, of which waited for: 4 -> 10; matrix products, arithmetic and copies ran while one was open for 14% -> 11% of each run, Pallas kernels for 0% -> 8%
where the time goes in v1:
time: 390 us; the launch traced here: 385 us
  waiting for transfers between devices  216 us (55%)
  starting transfers between devices  71 us (18%)
  local copies, waits for them, and re-layouts  61.3 us (16%)
  Pallas kernels  35.1 us (9%)
    all_to_all x4, waiting for transfers between devices, exchange(): lax.all_to_all(a.reshape(owners, PER, D), 'seq', split_axis=0, concat_axi...  63.2 us
    ppermute x2, waiting for transfers between devices, per_device(): theirs = beside_r(mine)  59.6 us
    ppermute x2, waiting for transfers between devices, per_device(): gate_w, up_w = (beside_w(gate), beside_w(up))  58.7 us
    all_to_all x4, starting transfers between devices, exchange(): lax.all_to_all(a.reshape(owners, PER, D), 'seq', split_axis=0, concat_axi...  43.3 us
    pallas_call x2, Pallas kernels, per_device(): call(hidden_body, (shape(rows, 2 * width),) * 2, [ANY] * 6, [pltpu.VMEM((...  18.8 us
    unnamed x35, local copies, waits for them, and re-layouts  18.7 us
    reshape x6, local copies, waits for them, and re-layouts, exchange(): return lax.all_to_all(a.reshape(owners, PER, D), 'seq', split_axis=0, con...  17.6 us
    ppermute x3, waiting for transfers between devices, shift(): return lax.ppermute(a, 'fsdp', [(i, (i + by) % 4) for i in range(4)])  15.3 us
  transfers between devices with their start and end apart: 18, of which 10 were waited for; matrix products, arithmetic and copies ran while one was open for 11% of the time, Pallas kernels for 8%

profile of v1, /device:TPU:1, one launch (start us, length us, event | category | flops | bytes accessed | tf_op | source)
XLA Modules:
  0.0 384.9 jit_solution(14421088277091978452)
XLA Ops:
  0.8 4.9 %collective-permute-start = (bf16[128,128]{1,0:T(8,128)(2,1)S(1)}, bf16[128,128]{1,0:T(8,128)(2,1)S(1)}, u32[]{:S(2)}, u32[]{:S(2)}) collective-permute-start(bf16[128,128]{1,0:T(8,128)(2,1)S(1)} %slice.9), channel_id=1, source_target_pairs={{0,4},{4,8},{8,12},{12,16},{16,20},{20,24},{24,28},{28,32},{32,36}... | collective-permute-start | bytes 98312 | tf_op jit(solution)/shard_map/ppermute | solution.py:167
  6.9 3.4 copy.24.ow_ref
  10.6 2.9 shard_map.100
  18.7 15.0 %collective-permute-done.1.r1 = bf16[64,2880]{1,0:T(8,128)(2,1)S(1)} collective-permute-done((bf16[64,2880]{1,0:T(8,128)(2,1)S(1)}, bf16[64,2880]{1,0:T(8,128)(2,1)S(1)}, u32[]{:S(2)}, u32[]{:S(2)}) %collective-permute-start.1) | collective-permute-done | bytes 368672 | tf_op jit(solution)/shard_map/ppermute | solution.py:165
  37.8 11.8 %all-to-all-start = ((bf16[64,4,2880]{2,1,0:T(4,128)(2,1)}), bf16[64,4,2880]{2,1,0:T(4,128)(2,1)}, u32[]{:S(2)}, u32[]{:S(2)}) async-start(bf16[64,4,2880]{2,1,0:T(4,128)(2,1)} %reshape.82), calls=%async_computation | async-start | bytes 3014656 | tf_op jit(solution)/shard_map/all_to_all | solution.py:209
  55.4 3.7 reshape.86
  59.1 28.9 %all-to-all-done = bf16[64,4,2880]{2,1,0:T(4,128)(2,1)} async-done(((bf16[64,4,2880]{2,1,0:T(4,128)(2,1)}), bf16[64,4,2880]{2,1,0:T(4,128)(2,1)}, u32[]{:S(2)}, u32[]{:S(2)}) %all-to-all-start) | async-done | bytes 1474592 | tf_op jit(solution)/shard_map/all_to_all | solution.py:209
  88.0 6.7 %all-to-all-start.2 = ((bf16[64,4,2880]{2,1,0:T(4,128)(2,1)}), bf16[64,4,2880]{2,1,0:T(4,128)(2,1)}, u32[]{:S(2)}, u32[]{:S(2)}) async-start(bf16[64,4,2880]{2,1,0:T(4,128)(2,1)} %reshape.86), calls=%async_computation.2 | async-start | bytes 3014656 | tf_op jit(solution)/shard_map/all_to_all | solution.py:209
  94.7 3.6 reshape.83.xo
  98.3 2.6 copy.27
  108.7 26.0 %collective-permute-done.4 = bf16[256,2880]{0,1:T(8,128)(2,1)} collective-permute-done((bf16[256,2880]{0,1:T(8,128)(2,1)}, bf16[256,2880]{0,1:T(8,128)(2,1)}, u32[]{:S(2)}, u32[]{:S(2)}) %collective-permute-start.4) | collective-permute-done | bytes 1474592 | tf_op jit(solution)/shard_map/ppermute | solution.py:224
  134.7 2.5 copy.28.xp
  137.3 11.3 %collective-permute-done.5.g1 = bf16[2880,384]{1,0:T(8,128)(2,1)} collective-permute-done((bf16[2880,384]{1,0:T(8,128)(2,1)}, bf16[2880,384]{1,0:T(8,128)(2,1)}, u32[]{:S(2)}, u32[]{:S(2)}) %collective-permute-start.5) | collective-permute-done | bytes 2211872 | tf_op jit(solution)/shard_map/ppermute | solution.py:170
  148.6 47.4 %collective-permute-done.6.u1 = bf16[2880,384]{1,0:T(8,128)(2,1)} collective-permute-done((bf16[2880,384]{1,0:T(8,128)(2,1)}, bf16[2880,384]{1,0:T(8,128)(2,1)}, u32[]{:S(2)}, u32[]{:S(2)}) %collective-permute-start.6) | collective-permute-done | bytes 2211872 | tf_op jit(solution)/shard_map/ppermute | solution.py:170
  200.4 9.4 %shard_map.103 = (bf16[256,768]{1,0:T(8,128)(2,1)S(1)}, bf16[256,768]{1,0:T(8,128)(2,1)S(1)}) custom-call(bf16[256,2880]{1,0:T(8,128)(2,1)S(1)} %copy-done.1, bf16[256,2880]{1,0:T(8,128)(2,1)S(1)} %copy-done.6, bf16[2880,384]{1,0:T(8,128)(2,1)S(1)} %bitcast.17, bf16[2880,384]{1,0:T(8,128)(2,1)} %bitcast.22, bf16[2880,384]{1,0:T(8,128)(2,1)} %collective-permute-done.5.g1, ...), custom_call_target="tpu_custom_call" | custom-call | flops 4529848320 | bytes 12582912 | tf_op jit(solution)/shard_map/pallas_call | solution.py:225
  209.9 9.8 %collective-permute-done.10 = bf16[1440,384]{1,0:T(8,128)(2,1)} collective-permute-done((bf16[1440,384]{1,0:T(8,128)(2,1)}, bf16[1440,384]{1,0:T(8,128)(2,1)}, u32[]{:S(2)}, u32[]{:S(2)}) %collective-permute-start.10) | collective-permute-done | bytes 1105952 | tf_op jit(solution)/shard_map/ppermute | solution.py:173
  223.9 5.0 %shard_map.104 = bf16[256,2880]{1,0:T(8,128)(2,1)S(1)} custom-call(bf16[256,768]{1,0:T(8,128)(2,1)S(1)} %get-tuple-element.28.ho, bf16[256,768]{1,0:T(8,128)(2,1)S(1)} %collective-permute-done.7.hr, bf16[2880,384]{1,0:T(8,128)(2,1)S(1)} %bitcast.14, bf16[2880,384]{1,0:T(8,128)(2,1)} %collective-permute-done.8.d1, ...), custom_call_target="tpu_custom_call" | custom-call | flops 2264924160 | bytes 12582912 | tf_op jit(solution)/shard_map/pallas_call | solution.py:238
  230.0 3.7 reshape.84
  233.8 11.8 %all-to-all-start.1 = ((bf16[64,4,2880]{2,1,0:T(4,128)(2,1)}), bf16[64,4,2880]{2,1,0:T(4,128)(2,1)}, u32[]{:S(2)}, u32[]{:S(2)}) async-start(bf16[64,4,2880]{2,1,0:T(4,128)(2,1)} %reshape.84), calls=%async_computation.1 | async-start | bytes 3014656 | tf_op jit(solution)/shard_map/all_to_all | solution.py:209
  245.6 3.6 reshape.87.xo
  249.2 2.6 copy.29
  251.8 8.5 %collective-permute-start.12 = (bf16[256,2880]{0,1:T(8,128)(2,1)}, bf16[256,2880]{0,1:T(8,128)(2,1)}, u32[]{:S(2)}, u32[]{:S(2)}) collective-permute-start(bf16[256,2880]{0,1:T(8,128)(2,1)} %copy.29), channel_id=1, source_target_pairs={{0,1},{1,0},{2,3},{3,2},{4,5},{5,4},{6,7},{7,6},{8,9},{9,8},{10,11... | collective-permute-start | bytes 4423688 | tf_op jit(solution)/shard_map/ppermute | solution.py:224
  260.2 33.6 %collective-permute-done.12 = bf16[256,2880]{0,1:T(8,128)(2,1)} collective-permute-done((bf16[256,2880]{0,1:T(8,128)(2,1)}, bf16[256,2880]{0,1:T(8,128)(2,1)}, u32[]{:S(2)}, u32[]{:S(2)}) %collective-permute-start.12) | collective-permute-done | bytes 1474592 | tf_op jit(solution)/shard_map/ppermute | solution.py:224
  293.9 2.6 copy.30.xp
  300.9 9.4 %shard_map.105 = (bf16[256,768]{1,0:T(8,128)(2,1)S(1)}, bf16[256,768]{1,0:T(8,128)(2,1)S(1)}) custom-call(bf16[256,2880]{1,0:T(8,128)(2,1)S(1)} %copy-done.2, bf16[256,2880]{1,0:T(8,128)(2,1)S(1)} %copy-done.7, bf16[2880,384]{1,0:T(8,128)(2,1)S(1)} %bitcast.18, bf16[2880,384]{1,0:T(8,128)(2,1)} %bitcast.23, bf16[2880,384]{1,0:T(8,128)(2,1)} %collective-permute-done.5.g1, ...), custom_call_target="tpu_custom_call" | custom-call | flops 4529848320 | bytes 12582912 | tf_op jit(solution)/shard_map/pallas_call | solution.py:225
  310.7 8.9 %collective-permute-done.13.hr = bf16[256,768]{1,0:T(8,128)(2,1)S(1)} collective-permute-done((bf16[256,768]{1,0:T(8,128)(2,1)S(1)}, bf16[256,768]{1,0:T(8,128)(2,1)S(1)}, u32[]{:S(2)}, u32[]{:S(2)}) %collective-permute-start.13) | collective-permute-done | bytes 393248 | tf_op jit(solution)/shard_map/ppermute | solution.py:237
  319.6 5.0 %shard_map.106 = bf16[256,2880]{1,0:T(8,128)(2,1)S(1)} custom-call(bf16[256,768]{1,0:T(8,128)(2,1)S(1)} %get-tuple-element.31.ho, bf16[256,768]{1,0:T(8,128)(2,1)S(1)} %collective-permute-done.13.hr, bf16[2880,384]{1,0:T(8,128)(2,1)S(1)} %bitcast.15, bf16[2880,384]{1,0:T(8,128)(2,1)} %collective-permute-done.8.d1, ...), custom_call_target="tpu_custom_call" | custom-call | flops 2264924160 | bytes 12582912 | tf_op jit(solution)/shard_map/pallas_call | solution.py:238
  325.7 3.7 reshape.88
  329.4 12.9 %all-to-all-start.3 = ((bf16[64,4,2880]{2,1,0:T(4,128)(2,1)}), bf16[64,4,2880]{2,1,0:T(4,128)(2,1)}, u32[]{:S(2)}, u32[]{:S(2)}) async-start(bf16[64,4,2880]{2,1,0:T(4,128)(2,1)} %reshape.88), calls=%async_computation.3 | async-start | bytes 3014656 | tf_op jit(solution)/shard_map/all_to_all | solution.py:209
  343.7 2.7 reshape.85.ret0
  346.3 34.4 %all-to-all-done.3 = bf16[64,4,2880]{2,1,0:T(4,128)(2,1)} async-done(((bf16[64,4,2880]{2,1,0:T(4,128)(2,1)}), bf16[64,4,2880]{2,1,0:T(4,128)(2,1)}, u32[]{:S(2)}, u32[]{:S(2)}) %all-to-all-start.3) | async-done | bytes 1474592 | tf_op jit(solution)/shard_map/all_to_all | solution.py:209
  380.7 2.6 reshape.89.ret1
  (81 shorter events, 43.3 us)
Async XLA Ops:
  0.8 9.8 %collective-permute-start = (bf16[128,128]{1,0:T(8,128)(2,1)S(1)}, bf16[128,128]{1,0:T(8,128)(2,1)S(1)}, u32[]{:S(2)}, u32[]{:S(2)}) collective-permute-start(bf16[128,128]{1,0:T(8,128)(2,1)S(1)} %slice.9), channel_id=1, source_target_pairs={{0,4},{4,8},{8,12},{12,16},{16,20},{20,24},{24,28},{28,32},{32,36}... | collective-permute-start | bytes 98312 | tf_op jit(solution)/shard_map/ppermute | solution.py:167
  6.9 3.4 copy-start.15
  6.9 3.7 copy-start.9
  6.9 3.7 copy-start.10
  10.6 23.4 %copy-start.8 = (bf16[64,2880]{1,0:T(8,128)(2,1)S(1)}, bf16[64,2880]{1,0:T(8,128)(2,1)}, u32[]{:S(2)}) copy-start(bf16[64,2880]{1,0:T(8,128)(2,1)} %hid.1) | copy-start | bytes 1105924
  13.5 20.1 %collective-permute-start.1 = (bf16[64,2880]{1,0:T(8,128)(2,1)S(1)}, bf16[64,2880]{1,0:T(8,128)(2,1)S(1)}, u32[]{:S(2)}, u32[]{:S(2)}) collective-permute-start(bf16[64,2880]{1,0:T(8,128)(2,1)S(1)} %get-tuple-element.20), channel_id=1, source_target_pairs={{0,1},{1,2},{2,3},{3,0},{4,5},{5,6},{6,7},{7,4},{8,9},{9,10},{10,1... | collective-permute-start | bytes 1105928 | tf_op jit(solution)/shard_map/ppermute | solution.py:165
  14.8 18.8 %collective-permute-start.2 = (bf16[64,2880]{1,0:T(8,128)(2,1)S(1)}, bf16[64,2880]{1,0:T(8,128)(2,1)S(1)}, u32[]{:S(2)}, u32[]{:S(2)}) collective-permute-start(bf16[64,2880]{1,0:T(8,128)(2,1)S(1)} %get-tuple-element.21), channel_id=1, source_target_pairs={{0,2},{1,3},{2,0},{3,1},{4,6},{5,7},{6,4},{7,5},{8,10},{9,11},{10,... | collective-permute-start | bytes 1105928 | tf_op jit(solution)/shard_map/ppermute | solution.py:165
  17.3 16.7 %collective-permute-start.3 = (bf16[64,2880]{1,0:T(8,128)(2,1)S(1)}, bf16[64,2880]{1,0:T(8,128)(2,1)S(1)}, u32[]{:S(2)}, u32[]{:S(2)}) collective-permute-start(bf16[64,2880]{1,0:T(8,128)(2,1)S(1)} %get-tuple-element.22), channel_id=1, source_target_pairs={{0,3},{1,0},{2,1},{3,2},{4,7},{5,4},{6,5},{7,6},{8,11},{9,8},{10,9... | collective-permute-start | bytes 1105928 | tf_op jit(solution)/shard_map/ppermute | solution.py:165
  35.2 1.2 copy-start.5
  37.8 11.9 %copy-start = (bf16[1,2880,384]{2,1,0:T(8,128)(2,1)S(1)}, bf16[1,2880,384]{2,1,0:T(8,128)(2,1)}, u32[]{:S(2)}) copy-start(bf16[1,2880,384]{2,1,0:T(8,128)(2,1)} %param.19) | copy-start | bytes 6635524
  37.8 50.2 %all-to-all-start = ((bf16[64,4,2880]{2,1,0:T(4,128)(2,1)}), bf16[64,4,2880]{2,1,0:T(4,128)(2,1)}, u32[]{:S(2)}, u32[]{:S(2)}) async-start(bf16[64,4,2880]{2,1,0:T(4,128)(2,1)} %reshape.82), calls=%async_computation | async-start | bytes 3014656 | tf_op jit(solution)/shard_map/all_to_all | solution.py:209
  49.6 52.6 %collective-permute-start.9 = (bf16[2880,384]{1,0:T(8,128)(2,1)S(1)}, bf16[2880,384]{1,0:T(8,128)(2,1)}, u32[]{:S(2)}, u32[]{:S(2)}) collective-permute-start(bf16[2880,384]{1,0:T(8,128)(2,1)S(1)} %bitcast.12), channel_id=1, source_target_pairs={{0,1},{1,0},{2,3},{3,2},{4,5},{5,4},{6,7},{7,6},{8,9},{9,8},{10,11... | collective-permute-start | bytes 6635528 | tf_op jit(solution)/shard_map/ppermute | solution.py:171
  51.1 55.1 %collective-permute-start.8 = (bf16[2880,384]{1,0:T(8,128)(2,1)S(1)}, bf16[2880,384]{1,0:T(8,128)(2,1)}, u32[]{:S(2)}, u32[]{:S(2)}) collective-permute-start(bf16[2880,384]{1,0:T(8,128)(2,1)S(1)} %bitcast.13), channel_id=1, source_target_pairs={{0,3},{3,0},{1,2},{2,1},{4,7},{7,4},{5,6},{6,5},{8,11},{11,8},{9,1... | collective-permute-start | bytes 6635528 | tf_op jit(solution)/shard_map/ppermute | solution.py:172
  52.7 95.9 %collective-permute-start.5 = (bf16[2880,384]{1,0:T(8,128)(2,1)}, bf16[2880,384]{1,0:T(8,128)(2,1)}, u32[]{:S(2)}, u32[]{:S(2)}) collective-permute-start(bf16[2880,384]{1,0:T(8,128)(2,1)} %bitcast.16), channel_id=1, source_target_pairs={{0,3},{3,0},{1,2},{2,1},{4,7},{7,4},{5,6},{6,5},{8,11},{11,8},{9,1... | collective-permute-start | bytes 6635528 | tf_op jit(solution)/shard_map/ppermute | solution.py:170
  53.8 142.2 %collective-permute-start.6 = (bf16[2880,384]{1,0:T(8,128)(2,1)}, bf16[2880,384]{1,0:T(8,128)(2,1)}, u32[]{:S(2)}, u32[]{:S(2)}) collective-permute-start(bf16[2880,384]{1,0:T(8,128)(2,1)} %bitcast.21), channel_id=1, source_target_pairs={{0,3},{3,0},{1,2},{2,1},{4,7},{7,4},{5,6},{6,5},{8,11},{11,8},{9,1... | collective-permute-start | bytes 6635528 | tf_op jit(solution)/shard_map/ppermute | solution.py:170
  88.0 145.8 %all-to-all-start.2 = ((bf16[64,4,2880]{2,1,0:T(4,128)(2,1)}), bf16[64,4,2880]{2,1,0:T(4,128)(2,1)}, u32[]{:S(2)}, u32[]{:S(2)}) async-start(bf16[64,4,2880]{2,1,0:T(4,128)(2,1)} %reshape.86), calls=%async_computation.2 | async-start | bytes 3014656 | tf_op jit(solution)/shard_map/all_to_all | solution.py:209
  100.9 33.8 %collective-permute-start.4 = (bf16[256,2880]{0,1:T(8,128)(2,1)}, bf16[256,2880]{0,1:T(8,128)(2,1)}, u32[]{:S(2)}, u32[]{:S(2)}) collective-permute-start(bf16[256,2880]{0,1:T(8,128)(2,1)} %copy.27), channel_id=1, source_target_pairs={{0,1},{1,0},{2,3},{3,2},{4,5},{5,4},{6,7},{7,6},{8,9},{9,8},{10,11... | collective-permute-start | bytes 4423688 | tf_op jit(solution)/shard_map/ppermute | solution.py:224
  104.6 115.1 %collective-permute-start.10 = (bf16[1440,384]{1,0:T(8,128)(2,1)}, bf16[1440,384]{1,0:T(8,128)(2,1)}, u32[]{:S(2)}, u32[]{:S(2)}) collective-permute-start(bf16[1440,384]{1,0:T(8,128)(2,1)} %slice.12), channel_id=1, source_target_pairs={{0,3},{3,0},{1,2},{2,1},{4,7},{7,4},{5,6},{6,5},{8,11},{11,8},{9,1... | collective-permute-start | bytes 3317768 | tf_op jit(solution)/shard_map/ppermute | solution.py:173
  108.6 112.5 %collective-permute-start.11 = (bf16[1440,384]{1,0:T(8,128)(2,1)}, bf16[1440,384]{1,0:T(8,128)(2,1)}, u32[]{:S(2)}, u32[]{:S(2)}) collective-permute-start(bf16[1440,384]{1,0:T(8,128)(2,1)} %slice.13), channel_id=1, source_target_pairs={{0,1},{1,0},{2,3},{3,2},{4,5},{5,4},{6,7},{7,6},{8,9},{9,8},{10,11... | collective-permute-start | bytes 3317768 | tf_op jit(solution)/shard_map/ppermute | solution.py:174
  196.0 1.4 copy-start.1
  197.4 1.4 copy-start.6
  198.8 1.6 copy-start.11
  209.8 12.7 %collective-permute-start.7 = (bf16[256,768]{1,0:T(8,128)(2,1)S(1)}, bf16[256,768]{1,0:T(8,128)(2,1)S(1)}, u32[]{:S(2)}, u32[]{:S(2)}) collective-permute-start(bf16[256,768]{1,0:T(8,128)(2,1)S(1)} %get-tuple-element.29), channel_id=1, source_target_pairs={{0,1},{1,0},{2,3},{3,2},{4,5},{5,4},{6,7},{7,6},{8,9},{9,8},{10,11... | collective-permute-start | bytes 1179656 | tf_op jit(solution)/shard_map/ppermute | solution.py:237
  222.6 1.4 copy-start.13
  233.8 95.7 %all-to-all-start.1 = ((bf16[64,4,2880]{2,1,0:T(4,128)(2,1)}), bf16[64,4,2880]{2,1,0:T(4,128)(2,1)}, u32[]{:S(2)}, u32[]{:S(2)}) async-start(bf16[64,4,2880]{2,1,0:T(4,128)(2,1)} %reshape.84), calls=%async_computation.1 | async-start | bytes 3014656 | tf_op jit(solution)/shard_map/all_to_all | solution.py:209
  251.8 42.1 %collective-permute-start.12 = (bf16[256,2880]{0,1:T(8,128)(2,1)}, bf16[256,2880]{0,1:T(8,128)(2,1)}, u32[]{:S(2)}, u32[]{:S(2)}) collective-permute-start(bf16[256,2880]{0,1:T(8,128)(2,1)} %copy.29), channel_id=1, source_target_pairs={{0,1},{1,0},{2,3},{3,2},{4,5},{5,4},{6,7},{7,6},{8,9},{9,8},{10,11... | collective-permute-start | bytes 4423688 | tf_op jit(solution)/shard_map/ppermute | solution.py:224
  296.5 1.4 copy-start.2
  297.8 1.4 copy-start.7
  299.2 1.6 copy-start.12
  310.3 9.3 %collective-permute-start.13 = (bf16[256,768]{1,0:T(8,128)(2,1)S(1)}, bf16[256,768]{1,0:T(8,128)(2,1)S(1)}, u32[]{:S(2)}, u32[]{:S(2)}) collective-permute-start(bf16[256,768]{1,0:T(8,128)(2,1)S(1)} %get-tuple-element.32), channel_id=1, source_target_pairs={{0,1},{1,0},{2,3},{3,2},{4,5},{5,4},{6,7},{7,6},{8,9},{9,8},{10,11... | collective-permute-start | bytes 1179656 | tf_op jit(solution)/shard_map/ppermute | solution.py:237
  329.4 13.0 %copy-start.14 = (bf16[2880,64]{0,1:T(8,128)(2,1)S(1)}, bf16[2880,64]{0,1:T(8,128)(2,1)}, u32[]{:S(2)}) copy-start(bf16[2880,64]{0,1:T(8,128)(2,1)} %param.15) | copy-start | bytes 1105924
  329.4 51.3 %all-to-all-start.3 = ((bf16[64,4,2880]{2,1,0:T(4,128)(2,1)}), bf16[64,4,2880]{2,1,0:T(4,128)(2,1)}, u32[]{:S(2)}, u32[]{:S(2)}) async-start(bf16[64,4,2880]{2,1,0:T(4,128)(2,1)} %reshape.88), calls=%async_computation.3 | async-start | bytes 3014656 | tf_op jit(solution)/shard_map/all_to_all | solution.py:209
  (2 other events, 2.2 us)
